TPU v7x, 32 devices: a whole 2x2x4 slice. The times are simulated.
32 devices in a mesh: dom: 16 (over z, y, x), tp: 2 (over core).
Axes of the slice: x: 2, y: 2, z: 4, core: 2. Of those that a mesh axis runs over, the one named last changes fastest.
Arguments:
- queries: bfloat16 [2, 256, 8192], P(None, 'dom', 'tp'), may hold values from -400 to 400
- new_kv: bfloat16 [2, 256, 2048], P(None, 'dom', 'tp'), may hold values from -5 to 5
- gen_cache: bfloat16 [256, 128, 2048], P('dom', None, 'tp'), may hold values from -5 to 5
- prompt_kv: bfloat16 [4096, 2048], P(None, 'tp'), may hold values from -5 to 5
- lengths: int32 [256], replicated, may hold values from 1 to 126
- ancestors: int32 [256], replicated, may hold values from 0 to 255, as said below
- tokens: int32 [2, 256], P(None, 'dom'), may hold values from 0 to 128255
- twist_vector: float32 [8192], P('tp'), may hold values from -31 to 31
- twist_bias: float32 [128256], replicated, may hold values from -5 to 5
- prior_weights: float32 [256], P('dom'), may hold values from -252 to 4
Outputs:
- twist: float32 [2, 256], P(None, 'dom')
- normalized: float32 [256], P('dom')
- resampled_cache: bfloat16 [256, 128, 2048], P('dom', None, 'tp')
- new_lengths: int32 [256], P('dom')
Inputs may be any that keep to these rules, and one draw needn't show every extreme that they name: Particle p's ancestor lies on the index of dom that holds p or at most 2 indices from it; the particles of one index of dom name at most 2 distinct ancestors on any other index, and exactly 2 for some pair of indices.
All inputs are finite; a program needn't handle non-finite values.
Results may differ from a plain program's by a relative error of at most 0.0018.
Values may be sent and summed in bfloat16 or wider, within the bound.
No kernel may reach another device: no remote copies, remote signals or barrier semaphores. Data moves between devices by JAX's collectives and lax.ppermute only.
A program may use at most 128 MiB of HBM per device.

v0:
```python
import functools
import math

import jax
import jax.numpy as jnp
from jax import lax
from jax.experimental import pallas as pl
from jax.experimental.pallas import tpu as pltpu
from jax.sharding import PartitionSpec as P

HEAD_DIM = 128
SPAN = 2
PICKS = 2
NEG_FILL = -1e30
KEY_CHUNK = 512
VMEM_BYTES = 50 * 1024 * 1024

ORDERS = ((-2, 2, 1, -1), (1, -1, -2, 2))


def with_new_rows(cache, new_rows, length, slot, per_dev):
    rows = cache.shape[0]
    row_ids = lax.broadcasted_iota(jnp.int32, (rows, 2 * per_dev), 0)
    col_ids = lax.broadcasted_iota(jnp.int32, (rows, 2 * per_dev), 1)
    step_ids = col_ids // per_dev
    hit = jnp.logical_and(col_ids - step_ids * per_dev == slot, row_ids == length + step_ids)
    placed = jnp.dot(
        hit.astype(jnp.bfloat16), new_rows, preferred_element_type=jnp.float32
    )
    old = lax.broadcasted_iota(jnp.int32, cache.shape, 0) < length
    return jnp.where(old, cache.astype(jnp.float32), placed).astype(jnp.bfloat16)


def named_range(anc_ref, reader, owner, per_dev, doms):
    safe = jnp.clip(reader, 0, doms - 1) * per_dev
    low, high = jnp.int32(per_dev), jnp.int32(-1)
    for j in range(per_dev):
        local = anc_ref[safe + j] - owner * per_dev
        named = jnp.logical_and(local >= 0, local < per_dev)
        low = jnp.minimum(low, jnp.where(named, local, per_dev))
        high = jnp.maximum(high, jnp.where(named, local, -1))
    return low, high


def pack_kernel(
    per_dev, doms, step_pairs, len_hbm, anc_hbm, new_ref, gen_ref, *refs
):
    sends = refs[: len(step_pairs)]
    new_len_ref, own_len_ref, len_ref, anc_ref, held, list_sem, in_sem, out_sem = refs[
        len(step_pairs) :
    ]
    lists = [
        pltpu.make_async_copy(anc_hbm, anc_ref, list_sem.at[0]),
        pltpu.make_async_copy(len_hbm, len_ref, list_sem.at[1]),
    ]
    for copy in lists:
        copy.start()
    me, odd = lax.axis_index("dom"), lax.axis_index("tp") % 2
    for copy in lists:
        copy.wait()
    picks = []
    loads = []
    for even_step, odd_step in step_pairs:
        reader = me + jnp.where(odd == 1, odd_step, even_step)
        low, high = named_range(anc_ref, reader, me, per_dev, doms)
        for pick in (jnp.minimum(low, per_dev - 1), jnp.maximum(high, 0)):
            k = len(picks)
            picks.append(pick)
            loads.append(pltpu.make_async_copy(gen_ref.at[pick], held.at[k], in_sem.at[k]))
            loads[-1].start()
    for j in range(per_dev):
        new_len_ref[j] = len_ref[anc_ref[me * per_dev + j]] + 2
        own_len_ref[j] = len_ref[me * per_dev + j]
    new_rows = new_ref[...].reshape(2 * per_dev, new_ref.shape[-1])
    stores = []
    for k, pick in enumerate(picks):
        loads[k].wait()
        held[k] = with_new_rows(
            held[k], new_rows, len_ref[me * per_dev + pick], pick, per_dev
        )
        stores.append(
            pltpu.make_async_copy(
                held.at[k], sends[k // PICKS].at[k % PICKS], out_sem.at[k]
            )
        )
        stores[-1].start()
    for store in stores:
        store.wait()


def pack(lengths, ancestors, new_kv, gen_cache, doms, step_pairs):
    per_dev, rows, width = gen_cache.shape
    count = len(step_pairs)
    smem = pl.BlockSpec(memory_space=pltpu.SMEM)
    vmem = pl.BlockSpec(memory_space=pltpu.VMEM)
    hbm = pl.BlockSpec(memory_space=pl.ANY)
    block_bytes = PICKS * rows * width * 2
    return pl.pallas_call(
        functools.partial(pack_kernel, per_dev, doms, step_pairs),
        out_shape=[jax.ShapeDtypeStruct((PICKS, rows, width), jnp.bfloat16)] * count
        + [jax.ShapeDtypeStruct((per_dev,), jnp.int32)] * 2,
        in_specs=[hbm, hbm, vmem, hbm],
        out_specs=[hbm] * count + [smem] * 2,
        scratch_shapes=[
            pltpu.SMEM(lengths.shape, jnp.int32),
            pltpu.SMEM(ancestors.shape, jnp.int32),
            pltpu.VMEM((count * PICKS, rows, width), jnp.bfloat16),
            pltpu.SemaphoreType.DMA((2,)),
            pltpu.SemaphoreType.DMA((count * PICKS,)),
            pltpu.SemaphoreType.DMA((count * PICKS,)),
        ],
        compiler_params=pltpu.CompilerParams(vmem_limit_bytes=VMEM_BYTES),
        cost_estimate=pl.CostEstimate(
            flops=0, bytes_accessed=2 * count * block_bytes, transcendentals=0
        ),
        name="pack_sends",
    )(lengths, ancestors, new_kv, gen_cache)


def tile_rows(block, count):
    return jnp.concatenate([block] * count, axis=0)


def attend_kernel(
    per_dev,
    group,
    len_ref,
    anc_ref,
    q_ref,
    prompt_ref,
    gen_ref,
    new_ref,
    head_ref,
    extra_ref,
    share_ref,
    out_ref,
    scores,
    grown,
    acc_ref,
):
    head = pl.program_id(0)
    me = lax.axis_index("dom")
    steps = q_ref.shape[0]
    rows = gen_ref.shape[1]
    keys = prompt_ref.shape[0]
    scale = 1.0 / math.sqrt(HEAD_DIM)
    base_rows = steps * per_dev
    all_rows = group * base_rows

    new_rows = new_ref[...].reshape(steps * per_dev, new_ref.shape[-1])
    for p in range(per_dev):
        grown[p] = with_new_rows(gen_ref[p], new_rows, len_ref[p], p, per_dev)
    for p in range(per_dev):
        local = jnp.clip(anc_ref[me * per_dev + p] - me * per_dev, 0, per_dev - 1)
        out_ref[p] = grown[local]

    q2 = q_ref[...].reshape(base_rows, group * HEAD_DIM)
    queries = jnp.concatenate(
        [q2[:, h * HEAD_DIM : (h + 1) * HEAD_DIM] for h in range(group)], axis=0
    )

    row_ids = lax.broadcasted_iota(jnp.int32, (base_rows, HEAD_DIM), 0)
    step_ids = row_ids // per_dev
    owner = row_ids - step_ids * per_dev
    last = step_ids
    for p in range(per_dev):
        last = last + jnp.where(owner == p, len_ref[p], 0)
    owner = tile_rows(owner, group)
    visible = tile_rows(lax.broadcasted_iota(jnp.int32, (base_rows, rows), 1) <= last, group)

    contract_last = (((1,), (1,)), ((), ()))
    own_scores = jnp.full((all_rows, rows), NEG_FILL, jnp.float32)
    for p in range(0, per_dev, 2):
        pair_keys = jnp.concatenate(
            [grown[p, :, :HEAD_DIM], grown[p + 1, :, :HEAD_DIM]], axis=0
        )
        pair = lax.dot_general(
            queries, pair_keys, contract_last, preferred_element_type=jnp.float32
        )
        own_scores = jnp.where(owner == p, pair[:, :rows], own_scores)
        own_scores = jnp.where(owner == p + 1, pair[:, rows:], own_scores)
    own_scores = jnp.where(visible, own_scores * scale, NEG_FILL)
    top = own_scores

    for first in range(0, keys, KEY_CHUNK):
        part = lax.dot_general(
            queries,
            prompt_ref[first : first + KEY_CHUNK, :HEAD_DIM],
            contract_last,
            preferred_element_type=jnp.float32,
        )
        part = part * scale
        scores[:, first : first + KEY_CHUNK] = part
        for k in range(0, KEY_CHUNK, HEAD_DIM):
            top = jnp.maximum(top, part[:, k : k + HEAD_DIM])
    row_max = jnp.broadcast_to(
        jnp.max(top, axis=1, keepdims=True), (all_rows, HEAD_DIM)
    )

    own_exp = jnp.where(visible, jnp.exp(own_scores - row_max), 0.0)
    total = own_exp
    mixed = jnp.zeros((all_rows, HEAD_DIM), jnp.float32)
    for p in range(0, per_dev, 2):
        pair_probs = jnp.concatenate(
            [jnp.where(owner == p + i, own_exp, 0.0).astype(jnp.bfloat16) for i in range(2)],
            axis=1,
        )
        pair_values = jnp.concatenate(
            [grown[p, :, HEAD_DIM:], grown[p + 1, :, HEAD_DIM:]], axis=0
        )
        mixed = mixed + jnp.dot(pair_probs, pair_values, preferred_element_type=jnp.float32)
    wide_max = jnp.concatenate([row_max] * (KEY_CHUNK // HEAD_DIM), axis=1)
    for first in range(0, keys, KEY_CHUNK):
        exps = jnp.exp(scores[:, first : first + KEY_CHUNK] - wide_max)
        for k in range(0, KEY_CHUNK, HEAD_DIM):
            total = total + exps[:, k : k + HEAD_DIM]
        mixed = mixed + jnp.dot(
            exps.astype(jnp.bfloat16),
            prompt_ref[first : first + KEY_CHUNK, HEAD_DIM:],
            preferred_element_type=jnp.float32,
        )
    mixed = mixed / jnp.sum(total, axis=1, keepdims=True)
    weighted = jnp.zeros((base_rows, HEAD_DIM), jnp.float32)
    for h in range(group):
        weighted = weighted + mixed[h * base_rows : (h + 1) * base_rows] * head_ref[0, h : h + 1, :]

    @pl.when(head == 0)
    def _():
        acc_ref[...] = weighted

    @pl.when(head > 0)
    def _():
        acc_ref[...] += weighted

    @pl.when(head == pl.num_programs(0) - 1)
    def _():
        padding = jnp.zeros((HEAD_DIM - base_rows, HEAD_DIM), jnp.float32)
        square = jnp.concatenate([acc_ref[...], padding], axis=0)
        row = jnp.sum(square.T, axis=0, keepdims=True) + extra_ref[...]
        share_ref[...] = jnp.broadcast_to(row[None], share_ref.shape)


def attend(
    own_lengths, ancestors, queries, prompt_kv, gen_cache, new_kv, twist_vector, extra, devices
):
    steps, per_dev, width = queries.shape
    keys, kv_width = prompt_kv.shape
    rows = gen_cache.shape[1]
    kv_local = kv_width // (2 * HEAD_DIM)
    group = width // (kv_local * HEAD_DIM)
    head_weights = twist_vector.reshape(kv_local, group, HEAD_DIM)
    smem = pl.BlockSpec(memory_space=pltpu.SMEM)
    pair = 2 * HEAD_DIM
    all_keys = keys + rows
    total_rows = steps * per_dev * group * kv_local
    return pl.pallas_call(
        functools.partial(attend_kernel, per_dev, group),
        grid=(kv_local,),
        out_shape=[
            jax.ShapeDtypeStruct((devices, 1, HEAD_DIM), jnp.float32),
            jax.ShapeDtypeStruct(gen_cache.shape, jnp.bfloat16),
        ],
        in_specs=[
            smem,
            smem,
            pl.BlockSpec((steps, per_dev, group * HEAD_DIM), lambda c: (0, 0, c)),
            pl.BlockSpec((keys, pair), lambda c: (0, c)),
            pl.BlockSpec((per_dev, rows, pair), lambda c: (0, 0, c)),
            pl.BlockSpec((steps, per_dev, pair), lambda c: (0, 0, c)),
            pl.BlockSpec((1, group, HEAD_DIM), lambda c: (c, 0, 0)),
            pl.BlockSpec((1, HEAD_DIM), lambda c: (0, 0)),
        ],
        out_specs=[
            pl.BlockSpec((devices, 1, HEAD_DIM), lambda c: (0, 0, 0)),
            pl.BlockSpec((per_dev, rows, pair), lambda c: (0, 0, c)),
        ],
        scratch_shapes=[
            pltpu.VMEM((group * steps * per_dev, keys), jnp.float32),
            pltpu.VMEM((per_dev, rows, pair), jnp.bfloat16),
            pltpu.VMEM((steps * per_dev, HEAD_DIM), jnp.float32),
        ],
        compiler_params=pltpu.CompilerParams(vmem_limit_bytes=VMEM_BYTES),
        cost_estimate=pl.CostEstimate(
            flops=4 * total_rows * all_keys * HEAD_DIM,
            bytes_accessed=2 * (prompt_kv.size + 2 * gen_cache.size),
            transcendentals=total_rows * all_keys,
        ),
        name="attend",
    )(own_lengths, ancestors, queries, prompt_kv, gen_cache, new_kv, head_weights, extra)


def deliver_kernel(
    per_dev, doms, steps, anc_ref, got_ref, held_ref, out_ref, block, in_sem, out_sem
):
    loads = [
        pltpu.make_async_copy(got_ref.at[k], block.at[k], in_sem.at[k]) for k in range(PICKS)
    ]
    for load in loads:
        load.start()
    me, odd = lax.axis_index("dom"), lax.axis_index("tp") % 2
    source = me - jnp.where(odd == 1, steps[1], steps[0])
    low, _ = named_range(anc_ref, me, source, per_dev, doms)
    for load in loads:
        load.wait()
    copies = []
    for p in range(per_dev):
        local = anc_ref[me * per_dev + p] - source * per_dev
        named = jnp.logical_and(local >= 0, local < per_dev)
        slot = jnp.where(local == low, 0, PICKS - 1)
        copy = pltpu.make_async_copy(block.at[slot], out_ref.at[p], out_sem.at[p])
        copies.append((named, copy))
        pl.when(named)(copy.start)
    for named, copy in copies:
        pl.when(named)(copy.wait)


def deliver(ancestors, got, held, steps, doms):
    per_dev = held.shape[0]
    smem = pl.BlockSpec(memory_space=pltpu.SMEM)
    hbm = pl.BlockSpec(memory_space=pl.ANY)
    return pl.pallas_call(
        functools.partial(deliver_kernel, per_dev, doms, steps),
        out_shape=jax.ShapeDtypeStruct(held.shape, held.dtype),
        in_specs=[smem, hbm, hbm],
        out_specs=hbm,
        input_output_aliases={2: 0},
        scratch_shapes=[
            pltpu.VMEM(got.shape, got.dtype),
            pltpu.SemaphoreType.DMA((PICKS,)),
            pltpu.SemaphoreType.DMA((per_dev,)),
        ],
        compiler_params=pltpu.CompilerParams(vmem_limit_bytes=VMEM_BYTES),
        cost_estimate=pl.CostEstimate(
            flops=0, bytes_accessed=2 * held.size // 2, transcendentals=0
        ),
        name="deliver",
    )(ancestors, got, held)


def normalize_kernel(doms, tps, per_dev, all_ref, twist_ref, normal_ref, sums):
    for d in range(doms):
        row = all_ref[d * tps]
        for t in range(1, tps):
            row = row + all_ref[d * tps + t]
        sums[d : d + 1, :] = row
    step_0, step_1, prior = (
        slice(k * per_dev, (k + 1) * per_dev) for k in range(3)
    )
    totals = sums[...]
    log_weights = totals[:, prior] + totals[:, step_1] - totals[:, step_0]
    largest = jnp.max(log_weights, keepdims=True)
    log_total = largest + jnp.log(jnp.sum(jnp.exp(log_weights - largest), keepdims=True))
    mine = sums[pl.ds(lax.axis_index("dom"), 1), :]
    own = mine[:, prior] + mine[:, step_1] - mine[:, step_0]
    twist_ref[...] = jnp.concatenate([mine[:, step_0], mine[:, step_1]], axis=0)
    normal_ref[...] = own - log_total


def normalize(shares, doms, tps, per_dev):
    return pl.pallas_call(
        functools.partial(normalize_kernel, doms, tps, per_dev),
        out_shape=[
            jax.ShapeDtypeStruct((2, per_dev), jnp.float32),
            jax.ShapeDtypeStruct((1, per_dev), jnp.float32),
        ],
        scratch_shapes=[pltpu.VMEM((doms, HEAD_DIM), jnp.float32)],
        name="normalize",
    )(shares)


def routes(doms, tps, steps):
    pairs = []
    for d in range(doms):
        for t in range(tps):
            target = d + steps[t % 2]
            if 0 <= target < doms:
                pairs.append((d * tps + t, target * tps + t))
    return pairs


def local(
    queries,
    new_kv,
    gen_cache,
    prompt_kv,
    lengths,
    ancestors,
    tokens,
    twist_vector,
    twist_bias,
    prior_weights,
):
    doms, tps = lax.axis_size("dom"), lax.axis_size("tp")
    per_dev = gen_cache.shape[0]
    step_pairs = list(zip(*ORDERS))
    everyone = ("dom", "tp")

    *first_sends, new_lengths, own_lengths = pack(
        lengths, ancestors, new_kv, gen_cache, doms, step_pairs[:1]
    )
    *later_sends, _, _ = pack(lengths, ancestors, new_kv, gen_cache, doms, step_pairs[1:])
    arrivals = [
        lax.ppermute(send, everyone, routes(doms, tps, steps))
        for send, steps in zip(first_sends + later_sends, step_pairs)
    ]

    bias = jnp.take(twist_bias, tokens, axis=0).reshape(-1)
    extra = jnp.concatenate([bias, prior_weights])
    extra = jnp.where(lax.axis_index("tp") == 0, extra, 0.0)
    extra = jnp.pad(extra, (0, HEAD_DIM - extra.size))[None]
    shares, resampled = attend(
        own_lengths,
        ancestors,
        queries,
        prompt_kv,
        gen_cache,
        new_kv,
        twist_vector,
        extra,
        doms * tps,
    )
    shares = lax.all_to_all(shares, everyone, 0, 0, tiled=True)
    twist, normalized = normalize(shares, doms, tps, per_dev)

    for got, steps in zip(arrivals, step_pairs):
        resampled = deliver(ancestors, got, resampled, steps, doms)
    return (twist, normalized.reshape(per_dev), resampled, new_lengths)


def solution(mesh):
    in_specs = (
        P(None, "dom", "tp"),
        P(None, "dom", "tp"),
        P("dom", None, "tp"),
        P(None, "tp"),
        P(),
        P(),
        P(None, "dom"),
        P("tp"),
        P(),
        P("dom"),
    )
    out_specs = (P(None, "dom"), P("dom"), P("dom", None, "tp"), P("dom"))
    return jax.shard_map(local, mesh=mesh, in_specs=in_specs, out_specs=out_specs, check_vma=False)
```

profile of v0, /device:TPU:0, one launch (start us, length us, event | category | flops | bytes accessed | tf_op | source)
XLA Modules:
  0.0 59.0 jit_solution(3842710956797801506)
XLA Ops:
  0.6 0.0 copy-start
  0.6 0.0 copy-start.1
  0.7 0.9 %copy-done.1 = bf16[2,16,1024]{2,1,0:T(8,128)(2,1)S(1)} copy-done((bf16[2,16,1024]{2,1,0:T(8,128)(2,1)S(1)}, bf16[2,16,1024]{2,1,0:T(8,128)(2,1)}, u32[]{:S(2)}) %copy-start.1) | copy-done | bytes 65560
  1.5 0.0 copy-start.4
  1.5 0.7 %copy-done.4 = s32[256]{0:T(256)S(1)} copy-done((s32[256]{0:T(256)S(1)}, s32[256]{0:T(256)}, u32[]{:S(2)}) %copy-start.4) | copy-done | bytes 1048
  2.2 0.0 copy-start.7
  2.2 0.7 %copy-done.7 = s32[256]{0:T(256)S(1)} copy-done((s32[256]{0:T(256)S(1)}, s32[256]{0:T(256)}, u32[]{:S(2)}) %copy-start.7) | copy-done | bytes 1048
  2.9 0.0 copy-start.8
  2.9 0.0 copy-start.9
  2.9 0.0 copy-start.2
  2.9 0.0 copy-start.3
  2.9 0.0 copy-start.5
  2.9 0.0 copy-start.6
  2.9 3.3 %pack_sends.2 = (bf16[2,128,1024]{2,1,0:T(8,128)(2,1)}, s32[16]{0:T(128)}, s32[16]{0:T(128)S(1)}) custom-call(s32[256]{0:T(256)S(1)} %copy-done.7, s32[256]{0:T(256)S(1)} %copy-done.4, bf16[2,16,1024]{2,1,0:T(8,128)(2,1)S(1)} %copy-done.1, bf16[16,128,1024]{2,1,0:T(8,128)(2,1)} %gen_ref.5), custom_call_target="tpu_custom_call" | custom-call | bytes 1048576 | tf_op jit(solution)/shard_map/pack_sends/pallas_call | solution.py:98
  6.3 1.3 %collective-permute-start.3 = (bf16[2,128,1024]{2,1,0:T(8,128)(2,1)}, bf16[2,128,1024]{2,1,0:T(8,128)(2,1)S(1)}, u32[]{:S(2)}, u32[]{:S(2)}) collective-permute-start(bf16[2,128,1024]{2,1,0:T(8,128)(2,1)} %get-tuple-element.21), channel_id=1, source_target_pairs={{1,3},{3,5},{4,0},{5,7},{6,2},{7,9},{8,4},{9,11},{10,6},{11,13},{1... | collective-permute-start | bytes 1572872 | tf_op jit(solution)/shard_map/ppermute | solution.py:403
  7.6 3.8 %pack_sends.3 = (bf16[2,128,1024]{2,1,0:T(8,128)(2,1)}, bf16[2,128,1024]{2,1,0:T(8,128)(2,1)}, bf16[2,128,1024]{2,1,0:T(8,128)(2,1)S(1)}, s32[16]{0:T(128)}, s32[16]{0:T(128)}) custom-call(s32[256]{0:T(256)S(1)} %copy-done.7, s32[256]{0:T(256)S(1)} %copy-done.4, bf16[2,16,1024]{2,1,0:T(8,128)(2,1)S(1)} %copy-done.1, bf16[16,128,1024]{2,1,0:T(8,128)(2,1)} %gen_ref.5), custom_call_target="tpu_custom_call" | custom-call | bytes 3145728 | tf_op jit(solution)/shard_map/pack_sends/pallas_call | solution.py:98
  11.3 5.5 %collective-permute-start.2 = (bf16[2,128,1024]{2,1,0:T(8,128)(2,1)}, bf16[2,128,1024]{2,1,0:T(8,128)(2,1)S(1)}, u32[]{:S(2)}, u32[]{:S(2)}) collective-permute-start(bf16[2,128,1024]{2,1,0:T(8,128)(2,1)} %get-tuple-element.20), channel_id=1, source_target_pairs={{0,4},{2,6},{3,1},{4,8},{5,3},{6,10},{7,5},{8,12},{9,7},{10,14},{1... | collective-permute-start | bytes 1572872 | tf_op jit(solution)/shard_map/ppermute | solution.py:403
  16.9 4.0 %collective-permute-start.1 = (bf16[2,128,1024]{2,1,0:T(8,128)(2,1)}, bf16[2,128,1024]{2,1,0:T(8,128)(2,1)S(1)}, u32[]{:S(2)}, u32[]{:S(2)}) collective-permute-start(bf16[2,128,1024]{2,1,0:T(8,128)(2,1)} %get-tuple-element.19), channel_id=1, source_target_pairs={{0,2},{2,4},{4,6},{5,1},{6,8},{7,3},{8,10},{9,5},{10,12},{11,7},{1... | collective-permute-start | bytes 1572872 | tf_op jit(solution)/shard_map/ppermute | solution.py:403
  20.8 1.3 %collective-permute-start = (bf16[2,128,1024]{2,1,0:T(8,128)(2,1)S(1)}, bf16[2,128,1024]{2,1,0:T(8,128)(2,1)S(1)}, u32[]{:S(2)}, u32[]{:S(2)}) collective-permute-start(bf16[2,128,1024]{2,1,0:T(8,128)(2,1)S(1)} %get-tuple-element.18), channel_id=1, source_target_pairs={{1,5},{2,0},{3,7},{4,2},{5,9},{6,4},{7,11},{8,6},{9,13},{10,8},{11... | collective-permute-start | bytes 1572872 | tf_op jit(solution)/shard_map/ppermute | solution.py:403
  22.1 0.0 copy-done.8
  22.1 0.1 reshape.28
  22.2 0.0 copy-done
  22.2 0.7 %gather_fusion = f32[32]{0:T(128)S(1)} fusion(f32[128256]{0:T(1024)S(1)} %copy-done, s32[1024]{0:T(1024)S(1)} %pad_clamp_fusion), kind=kCustom, calls=%fused_computation | custom fusion | bytes 384 | tf_op jit(solution)/shard_map/jit(_take)/gather | solution.py:407
  22.9 0.1 reshape.27
  23.0 0.1 select_n.24
  23.1 0.0 copy-done.9
  23.1 0.1 broadcast_select_fusion
  23.2 0.0 copy-done.2
  23.2 0.0 copy-done.3
  23.2 0.0 copy-done.5
  23.2 0.0 copy-done.6
  23.2 15.1 %attend.1 = (f32[32,1,128]{2,1,0:T(1,128)S(1)}, bf16[16,128,1024]{2,1,0:T(8,128)(2,1)}) custom-call(s32[16]{0:T(128)S(1)} %get-tuple-element.14.len_ref, s32[256]{0:T(256)S(1)} %copy-done.5, bf16[2,16,4096]{2,1,0:T(8,128)(2,1)S(1)} %copy-done.3, bf16[4096,1024]{1,0:T(8,128)(2,1)} %prompt_ref.1, bf16[16,128,1024]{2,1,0:T(8,128)(2,1)} %gen_ref.5, ...), custom_call_target="tpu_custom_call" | custom-call | flops 2214592512 | bytes 16777216 | tf_op jit(solution)/shard_map/attend/pallas_call | solution.py:256
  38.3 14.0 %all_to_all.5.all_ref = f32[32,1,128]{2,1,0:T(1,128)} all-to-all(f32[32,1,128]{2,1,0:T(1,128)S(1)} %get-tuple-element.15), channel_id=1, replica_groups=mesh['dom'=16,'tp'=2] {'dom','tp'}, dimensions={0} | all-to-all | bytes 32768 | tf_op jit(solution)/shard_map/all_to_all | solution.py:422
  52.3 1.7 %normalize.1 = (f32[2,16]{1,0:T(2,128)}, f32[1,16]{1,0:T(1,128)}) custom-call(f32[32,1,128]{2,1,0:T(1,128)} %all_to_all.5.all_ref), custom_call_target="tpu_custom_call" | custom-call | tf_op jit(solution)/shard_map/normalize/pallas_call | solution.py:360
  54.0 0.0 collective-permute-done.3.got_ref
  54.0 1.7 %deliver.4.held_ref = bf16[16,128,1024]{2,1,0:T(8,128)(2,1)} custom-call(s32[256]{0:T(256)S(1)} %copy-done.5, bf16[2,128,1024]{2,1,0:T(8,128)(2,1)S(1)} %collective-permute-done.3.got_ref, bf16[16,128,1024]{2,1,0:T(8,128)(2,1)} %get-tuple-element.22.held_ref), custom_call_target="tpu_custom_call", output_to_operand_aliasing={{}: (2, {})} | custom-call | bytes 2097152 | tf_op jit(solution)/shard_map/deliver/pallas_call | solution.py:321
  55.7 0.0 collective-permute-done.2.got_ref
  55.7 0.9 %deliver.5.held_ref = bf16[16,128,1024]{2,1,0:T(8,128)(2,1)} custom-call(s32[256]{0:T(256)S(1)} %copy-done.5, bf16[2,128,1024]{2,1,0:T(8,128)(2,1)S(1)} %collective-permute-done.2.got_ref, bf16[16,128,1024]{2,1,0:T(8,128)(2,1)} %deliver.4.held_ref), custom_call_target="tpu_custom_call", output_to_operand_aliasing={{}: (2, {})} | custom-call | bytes 2097152 | tf_op jit(solution)/shard_map/deliver/pallas_call | solution.py:321
  56.6 0.0 collective-permute-done.1.got_ref
  56.6 0.9 %deliver.6.held_ref = bf16[16,128,1024]{2,1,0:T(8,128)(2,1)} custom-call(s32[256]{0:T(256)S(1)} %copy-done.5, bf16[2,128,1024]{2,1,0:T(8,128)(2,1)S(1)} %collective-permute-done.1.got_ref, bf16[16,128,1024]{2,1,0:T(8,128)(2,1)} %deliver.5.held_ref), custom_call_target="tpu_custom_call", output_to_operand_aliasing={{}: (2, {})} | custom-call | bytes 2097152 | tf_op jit(solution)/shard_map/deliver/pallas_call | solution.py:321
  57.5 0.0 collective-permute-done.got_ref
  57.5 1.5 %deliver.7 = bf16[16,128,1024]{2,1,0:T(8,128)(2,1)} custom-call(s32[256]{0:T(256)S(1)} %copy-done.5, bf16[2,128,1024]{2,1,0:T(8,128)(2,1)S(1)} %collective-permute-done.got_ref, bf16[16,128,1024]{2,1,0:T(8,128)(2,1)} %deliver.6.held_ref), custom_call_target="tpu_custom_call", output_to_operand_aliasing={{}: (2, {})} | custom-call | bytes 2097152 | tf_op jit(solution)/shard_map/deliver/pallas_call | solution.py:321
  (4 shorter events, 0.0 us)
Async XLA Ops:
  0.6 21.6 %copy-start = (f32[128256]{0:T(1024)S(1)}, f32[128256]{0:T(1024)}, u32[]{:S(2)}) copy-start(f32[128256]{0:T(1024)} %param.18) | copy-start | bytes 1539076
  0.6 0.9 %copy-start.1 = (bf16[2,16,1024]{2,1,0:T(8,128)(2,1)S(1)}, bf16[2,16,1024]{2,1,0:T(8,128)(2,1)}, u32[]{:S(2)}) copy-start(bf16[2,16,1024]{2,1,0:T(8,128)(2,1)} %new_ref.5) | copy-start | bytes 196612
  1.5 0.7 %copy-start.4 = (s32[256]{0:T(256)S(1)}, s32[256]{0:T(256)}, u32[]{:S(2)}) copy-start(s32[256]{0:T(256)} %anc_ref.9) | copy-start | bytes 3076
  2.2 0.7 %copy-start.7 = (s32[256]{0:T(256)S(1)}, s32[256]{0:T(256)}, u32[]{:S(2)}) copy-start(s32[256]{0:T(256)} %len_hbm.3) | copy-start | bytes 3076
  2.9 19.2 %copy-start.8 = (s32[2,16]{1,0:T(2,128)S(1)}, s32[2,16]{1,0:T(2,128)}, u32[]{:S(2)}) copy-start(s32[2,16]{1,0:T(2,128)} %param.16) | copy-start | bytes 388
  2.9 20.2 %copy-start.9 = (f32[16]{0:T(128)S(1)}, f32[16]{0:T(128)}, u32[]{:S(2)}) copy-start(f32[16]{0:T(128)} %param.19) | copy-start | bytes 196
  2.9 20.3 %copy-start.2 = (bf16[2,16,1024]{2,1,0:T(8,128)(2,1)S(1)}, bf16[2,16,1024]{2,1,0:T(8,128)(2,1)}, u32[]{:S(2)}) copy-start(bf16[2,16,1024]{2,1,0:T(8,128)(2,1)} %new_ref.5) | copy-start | bytes 196612
  2.9 20.3 %copy-start.3 = (bf16[2,16,4096]{2,1,0:T(8,128)(2,1)S(1)}, bf16[2,16,4096]{2,1,0:T(8,128)(2,1)}, u32[]{:S(2)}) copy-start(bf16[2,16,4096]{2,1,0:T(8,128)(2,1)} %q_ref.1) | copy-start | bytes 786436
  2.9 20.3 %copy-start.5 = (s32[256]{0:T(256)S(1)}, s32[256]{0:T(256)}, u32[]{:S(2)}) copy-start(s32[256]{0:T(256)} %anc_ref.9) | copy-start | bytes 3076
  2.9 20.3 %copy-start.6 = (f32[4096]{0:T(1024)S(1)}, f32[4096]{0:T(1024)}, u32[]{:S(2)}) copy-start(f32[4096]{0:T(1024)} %param.17) | copy-start | bytes 49156
  6.3 47.7 %collective-permute-start.3 = (bf16[2,128,1024]{2,1,0:T(8,128)(2,1)}, bf16[2,128,1024]{2,1,0:T(8,128)(2,1)S(1)}, u32[]{:S(2)}, u32[]{:S(2)}) collective-permute-start(bf16[2,128,1024]{2,1,0:T(8,128)(2,1)} %get-tuple-element.21), channel_id=1, source_target_pairs={{1,3},{3,5},{4,0},{5,7},{6,2},{7,9},{8,4},{9,11},{10,6},{11,13},{1... | collective-permute-start | bytes 1572872 | tf_op jit(solution)/shard_map/ppermute | solution.py:403
  11.3 44.3 %collective-permute-start.2 = (bf16[2,128,1024]{2,1,0:T(8,128)(2,1)}, bf16[2,128,1024]{2,1,0:T(8,128)(2,1)S(1)}, u32[]{:S(2)}, u32[]{:S(2)}) collective-permute-start(bf16[2,128,1024]{2,1,0:T(8,128)(2,1)} %get-tuple-element.20), channel_id=1, source_target_pairs={{0,4},{2,6},{3,1},{4,8},{5,3},{6,10},{7,5},{8,12},{9,7},{10,14},{1... | collective-permute-start | bytes 1572872 | tf_op jit(solution)/shard_map/ppermute | solution.py:403
  16.9 39.7 %collective-permute-start.1 = (bf16[2,128,1024]{2,1,0:T(8,128)(2,1)}, bf16[2,128,1024]{2,1,0:T(8,128)(2,1)S(1)}, u32[]{:S(2)}, u32[]{:S(2)}) collective-permute-start(bf16[2,128,1024]{2,1,0:T(8,128)(2,1)} %get-tuple-element.19), channel_id=1, source_target_pairs={{0,2},{2,4},{4,6},{5,1},{6,8},{7,3},{8,10},{9,5},{10,12},{11,7},{1... | collective-permute-start | bytes 1572872 | tf_op jit(solution)/shard_map/ppermute | solution.py:403
  20.8 36.7 %collective-permute-start = (bf16[2,128,1024]{2,1,0:T(8,128)(2,1)S(1)}, bf16[2,128,1024]{2,1,0:T(8,128)(2,1)S(1)}, u32[]{:S(2)}, u32[]{:S(2)}) collective-permute-start(bf16[2,128,1024]{2,1,0:T(8,128)(2,1)S(1)} %get-tuple-element.18), channel_id=1, source_target_pairs={{1,5},{2,0},{3,7},{4,2},{5,9},{6,4},{7,11},{8,6},{9,13},{10,8},{11... | collective-permute-start | bytes 1572872 | tf_op jit(solution)/shard_map/ppermute | solution.py:403
where the time goes:
time: 59.4 us; the launch traced here: 59 us
  Pallas kernels  28.9 us (49%)
  blocking collectives  14 us (24%)
  starting transfers between devices  12 us (20%)
  local copies, waits for them, and re-layouts  3.23 us (5%)
  between operations  0.81 us (1%)
    pallas_call x1, Pallas kernels, attend(): pl.pallas_call(functools.partial(attend_kernel, per_dev, group), grid=(kv...  15.1 us
    all_to_all x1, blocking collectives, local(): shares = lax.all_to_all(shares, everyone, 0, 0, tiled=True)  14 us
    ppermute x4, starting transfers between devices, local(): lax.ppermute(send, everyone, routes(doms, tps, steps))  12 us
    pallas_call x2, Pallas kernels, pack(): pl.pallas_call(functools.partial(pack_kernel, per_dev, doms, step_pairs),...  7.09 us
    pallas_call x4, Pallas kernels, deliver(): pl.pallas_call(functools.partial(deliver_kernel, per_dev, doms, steps), o...  4.99 us
    unnamed x20, local copies, waits for them, and re-layouts  2.28 us
    pallas_call x1, Pallas kernels, normalize(): pl.pallas_call(functools.partial(normalize_kernel, doms, tps, per_dev), o...  1.7 us
  transfers between devices with their start and end apart: 4, of which 0 were waited for; matrix products, arithmetic and copies ran while one was open for 2% of the time, Pallas kernels for 41%

commit v1 on v0

--- a/solution.py
+++ b/solution.py
@@ -13,79 +13,82 @@
 PICKS = 2
 NEG_FILL = -1e30
 KEY_CHUNK = 512
-VMEM_BYTES = 50 * 1024 * 1024
+VMEM_BYTES = 44 * 1024 * 1024
+ROW_TILE = 16
+WINDOW = 2 * ROW_TILE
 
 ORDERS = ((-2, 2, 1, -1), (1, -1, -2, 2))
 
 
-def with_new_rows(cache, new_rows, length, slot, per_dev):
-    rows = cache.shape[0]
-    row_ids = lax.broadcasted_iota(jnp.int32, (rows, 2 * per_dev), 0)
-    col_ids = lax.broadcasted_iota(jnp.int32, (rows, 2 * per_dev), 1)
-    step_ids = col_ids // per_dev
-    hit = jnp.logical_and(col_ids - step_ids * per_dev == slot, row_ids == length + step_ids)
-    placed = jnp.dot(
-        hit.astype(jnp.bfloat16), new_rows, preferred_element_type=jnp.float32
-    )
-    old = lax.broadcasted_iota(jnp.int32, cache.shape, 0) < length
-    return jnp.where(old, cache.astype(jnp.float32), placed).astype(jnp.bfloat16)
-
-
-def named_range(anc_ref, reader, owner, per_dev, doms):
-    safe = jnp.clip(reader, 0, doms - 1) * per_dev
+def in_hbm(x):
+    return pltpu.with_memory_space_constraint(x, pltpu.HBM)
+
+
+def place_new_rows(cache, new_rows, length, slot, per_dev):
+    rows, width = cache.shape
+    first = pl.multiple_of(
+        jnp.minimum(length // ROW_TILE * ROW_TILE, rows - WINDOW), ROW_TILE
+    )
+    row_ids = first + lax.broadcasted_iota(jnp.int32, (WINDOW, width), 0)
+    old = cache[pl.ds(first, WINDOW), :].astype(jnp.float32)
+    later = jnp.where(row_ids == length + 1, new_rows[pl.ds(per_dev + slot, 1), :], 0.0)
+    later = jnp.where(row_ids == length, new_rows[pl.ds(slot, 1), :], later)
+    cache[pl.ds(first, WINDOW), :] = jnp.where(row_ids < length, old, later).astype(
+        jnp.bfloat16
+    )
+
+    def clear(tile, carry):
+        start = pl.multiple_of(tile * ROW_TILE, ROW_TILE)
+        cache[pl.ds(start, ROW_TILE), :] = jnp.zeros((ROW_TILE, width), jnp.bfloat16)
+        return carry
+
+    lax.fori_loop(first // ROW_TILE + WINDOW // ROW_TILE, rows // ROW_TILE, clear, 0)
+
+
+def named_range(anc_ref, first, owner, per_dev):
     low, high = jnp.int32(per_dev), jnp.int32(-1)
     for j in range(per_dev):
-        local = anc_ref[safe + j] - owner * per_dev
+        local = anc_ref[first + j] - owner * per_dev
         named = jnp.logical_and(local >= 0, local < per_dev)
         low = jnp.minimum(low, jnp.where(named, local, per_dev))
         high = jnp.maximum(high, jnp.where(named, local, -1))
     return low, high
 
 
-def pack_kernel(
-    per_dev, doms, step_pairs, len_hbm, anc_hbm, new_ref, gen_ref, *refs
-):
+def pack_kernel(per_dev, doms, step_pairs, len_hbm, anc_hbm, new_hbm, gen_hbm, *refs):
     sends = refs[: len(step_pairs)]
-    new_len_ref, own_len_ref, len_ref, anc_ref, held, list_sem, in_sem, out_sem = refs[
-        len(step_pairs) :
-    ]
+    new_len_ref, own_len_ref, own_anc_ref = refs[len(step_pairs) : len(step_pairs) + 3]
+    len_ref, anc_ref, new_bf16, new_rows, list_sem, load_sem = refs[len(step_pairs) + 3 :]
     lists = [
         pltpu.make_async_copy(anc_hbm, anc_ref, list_sem.at[0]),
         pltpu.make_async_copy(len_hbm, len_ref, list_sem.at[1]),
+        pltpu.make_async_copy(new_hbm, new_bf16, list_sem.at[2]),
     ]
     for copy in lists:
         copy.start()
     me, odd = lax.axis_index("dom"), lax.axis_index("tp") % 2
-    for copy in lists:
-        copy.wait()
+    lists[0].wait()
     picks = []
     loads = []
-    for even_step, odd_step in step_pairs:
-        reader = me + jnp.where(odd == 1, odd_step, even_step)
-        low, high = named_range(anc_ref, reader, me, per_dev, doms)
-        for pick in (jnp.minimum(low, per_dev - 1), jnp.maximum(high, 0)):
-            k = len(picks)
-            picks.append(pick)
-            loads.append(pltpu.make_async_copy(gen_ref.at[pick], held.at[k], in_sem.at[k]))
-            loads[-1].start()
+    for k, (even_step, odd_step) in enumerate(step_pairs):
+        reader = jnp.clip(me + jnp.where(odd == 1, odd_step, even_step), 0, doms - 1)
+        low, high = named_range(anc_ref, reader * per_dev, me, per_dev)
+        for i, pick in enumerate((jnp.minimum(low, per_dev - 1), jnp.maximum(high, 0))):
+            target = sends[k].at[i]
+            load = pltpu.make_async_copy(gen_hbm.at[pick], target, load_sem.at[len(loads)])
+            load.start()
+            picks.append((pick, target))
+            loads.append(load)
+    lists[1].wait()
     for j in range(per_dev):
+        own_anc_ref[j] = anc_ref[me * per_dev + j]
         new_len_ref[j] = len_ref[anc_ref[me * per_dev + j]] + 2
         own_len_ref[j] = len_ref[me * per_dev + j]
-    new_rows = new_ref[...].reshape(2 * per_dev, new_ref.shape[-1])
-    stores = []
-    for k, pick in enumerate(picks):
-        loads[k].wait()
-        held[k] = with_new_rows(
-            held[k], new_rows, len_ref[me * per_dev + pick], pick, per_dev
-        )
-        stores.append(
-            pltpu.make_async_copy(
-                held.at[k], sends[k // PICKS].at[k % PICKS], out_sem.at[k]
-            )
-        )
-        stores[-1].start()
-    for store in stores:
-        store.wait()
+    lists[2].wait()
+    new_rows[...] = new_bf16[...].astype(jnp.float32).reshape(new_rows.shape)
+    for load, (pick, target) in zip(loads, picks):
+        load.wait()
+        place_new_rows(target, new_rows, len_ref[me * per_dev + pick], pick, per_dev)
 
 
 def pack(lengths, ancestors, new_kv, gen_cache, doms, step_pairs):
@@ -93,20 +96,20 @@
     count = len(step_pairs)
     smem = pl.BlockSpec(memory_space=pltpu.SMEM)
     vmem = pl.BlockSpec(memory_space=pltpu.VMEM)
-    hbm = pl.BlockSpec(memory_space=pl.ANY)
+    hbm = pl.BlockSpec(memory_space=pltpu.HBM)
     block_bytes = PICKS * rows * width * 2
     return pl.pallas_call(
         functools.partial(pack_kernel, per_dev, doms, step_pairs),
         out_shape=[jax.ShapeDtypeStruct((PICKS, rows, width), jnp.bfloat16)] * count
-        + [jax.ShapeDtypeStruct((per_dev,), jnp.int32)] * 2,
-        in_specs=[hbm, hbm, vmem, hbm],
-        out_specs=[hbm] * count + [smem] * 2,
+        + [jax.ShapeDtypeStruct((per_dev,), jnp.int32)] * 3,
+        in_specs=[hbm] * 4,
+        out_specs=[vmem] * count + [smem] * 3,
         scratch_shapes=[
             pltpu.SMEM(lengths.shape, jnp.int32),
             pltpu.SMEM(ancestors.shape, jnp.int32),
-            pltpu.VMEM((count * PICKS, rows, width), jnp.bfloat16),
-            pltpu.SemaphoreType.DMA((2,)),
-            pltpu.SemaphoreType.DMA((count * PICKS,)),
+            pltpu.VMEM(new_kv.shape, jnp.bfloat16),
+            pltpu.VMEM((2 * per_dev, width), jnp.float32),
+            pltpu.SemaphoreType.DMA((3,)),
             pltpu.SemaphoreType.DMA((count * PICKS,)),
         ],
         compiler_params=pltpu.CompilerParams(vmem_limit_bytes=VMEM_BYTES),
@@ -114,7 +117,7 @@
             flops=0, bytes_accessed=2 * count * block_bytes, transcendentals=0
         ),
         name="pack_sends",
-    )(lengths, ancestors, new_kv, gen_cache)
+    )(*(in_hbm(x) for x in (lengths, ancestors, new_kv, gen_cache)))
 
 
 def tile_rows(block, count):
@@ -136,6 +139,7 @@
     out_ref,
     scores,
     grown,
+    new_rows,
     acc_ref,
 ):
     head = pl.program_id(0)
@@ -147,11 +151,12 @@
     base_rows = steps * per_dev
     all_rows = group * base_rows
 
-    new_rows = new_ref[...].reshape(steps * per_dev, new_ref.shape[-1])
+    new_rows[...] = new_ref[...].astype(jnp.float32).reshape(new_rows.shape)
     for p in range(per_dev):
-        grown[p] = with_new_rows(gen_ref[p], new_rows, len_ref[p], p, per_dev)
+        grown[p] = gen_ref[p]
+        place_new_rows(grown.at[p], new_rows, len_ref[p], p, per_dev)
     for p in range(per_dev):
-        local = jnp.clip(anc_ref[me * per_dev + p] - me * per_dev, 0, per_dev - 1)
+        local = jnp.clip(anc_ref[p] - me * per_dev, 0, per_dev - 1)
         out_ref[p] = grown[local]
 
     q2 = q_ref[...].reshape(base_rows, group * HEAD_DIM)
@@ -241,7 +246,7 @@
 
 
 def attend(
-    own_lengths, ancestors, queries, prompt_kv, gen_cache, new_kv, twist_vector, extra, devices
+    own_lengths, own_ancestors, queries, prompt_kv, gen_cache, new_kv, twist_vector, extra, devices
 ):
     steps, per_dev, width = queries.shape
     keys, kv_width = prompt_kv.shape
@@ -277,6 +282,7 @@
         scratch_shapes=[
             pltpu.VMEM((group * steps * per_dev, keys), jnp.float32),
             pltpu.VMEM((per_dev, rows, pair), jnp.bfloat16),
+            pltpu.VMEM((steps * per_dev, pair), jnp.float32),
             pltpu.VMEM((steps * per_dev, HEAD_DIM), jnp.float32),
         ],
         compiler_params=pltpu.CompilerParams(vmem_limit_bytes=VMEM_BYTES),
@@ -286,58 +292,29 @@
             transcendentals=total_rows * all_keys,
         ),
         name="attend",
-    )(own_lengths, ancestors, queries, prompt_kv, gen_cache, new_kv, head_weights, extra)
-
-
-def deliver_kernel(
-    per_dev, doms, steps, anc_ref, got_ref, held_ref, out_ref, block, in_sem, out_sem
-):
-    loads = [
-        pltpu.make_async_copy(got_ref.at[k], block.at[k], in_sem.at[k]) for k in range(PICKS)
-    ]
-    for load in loads:
-        load.start()
+    )(own_lengths, own_ancestors, queries, prompt_kv, gen_cache, new_kv, head_weights, extra)
+
+
+def start_delivery(per_dev, step_pairs, anc_ref, gots, out_ref, sem):
     me, odd = lax.axis_index("dom"), lax.axis_index("tp") % 2
-    source = me - jnp.where(odd == 1, steps[1], steps[0])
-    low, _ = named_range(anc_ref, me, source, per_dev, doms)
-    for load in loads:
-        load.wait()
     copies = []
-    for p in range(per_dev):
-        local = anc_ref[me * per_dev + p] - source * per_dev
-        named = jnp.logical_and(local >= 0, local < per_dev)
-        slot = jnp.where(local == low, 0, PICKS - 1)
-        copy = pltpu.make_async_copy(block.at[slot], out_ref.at[p], out_sem.at[p])
-        copies.append((named, copy))
-        pl.when(named)(copy.start)
-    for named, copy in copies:
-        pl.when(named)(copy.wait)
-
-
-def deliver(ancestors, got, held, steps, doms):
-    per_dev = held.shape[0]
-    smem = pl.BlockSpec(memory_space=pltpu.SMEM)
-    hbm = pl.BlockSpec(memory_space=pl.ANY)
-    return pl.pallas_call(
-        functools.partial(deliver_kernel, per_dev, doms, steps),
-        out_shape=jax.ShapeDtypeStruct(held.shape, held.dtype),
-        in_specs=[smem, hbm, hbm],
-        out_specs=hbm,
-        input_output_aliases={2: 0},
-        scratch_shapes=[
-            pltpu.VMEM(got.shape, got.dtype),
-            pltpu.SemaphoreType.DMA((PICKS,)),
-            pltpu.SemaphoreType.DMA((per_dev,)),
-        ],
-        compiler_params=pltpu.CompilerParams(vmem_limit_bytes=VMEM_BYTES),
-        cost_estimate=pl.CostEstimate(
-            flops=0, bytes_accessed=2 * held.size // 2, transcendentals=0
-        ),
-        name="deliver",
-    )(ancestors, got, held)
-
-
-def normalize_kernel(doms, tps, per_dev, all_ref, twist_ref, normal_ref, sums):
+    for k, (got, steps) in enumerate(zip(gots, step_pairs)):
+        source = me - jnp.where(odd == 1, steps[1], steps[0])
+        low, _ = named_range(anc_ref, 0, source, per_dev)
+        for p in range(per_dev):
+            local = anc_ref[p] - source * per_dev
+            named = jnp.logical_and(local >= 0, local < per_dev)
+            slot = jnp.where(local == low, 0, PICKS - 1)
+            copy = pltpu.make_async_copy(got.at[slot], out_ref.at[p], sem.at[k, p])
+            copies.append((named, copy))
+            pl.when(named)(copy.start)
+    return copies
+
+
+def finish_kernel(per_dev, doms, tps, step_pairs, anc_ref, *refs):
+    gots = refs[: len(step_pairs)]
+    _, all_ref, out_ref, twist_ref, normal_ref, sums, sem = refs[len(step_pairs) :]
+    copies = start_delivery(per_dev, step_pairs, anc_ref, gots, out_ref, sem)
     for d in range(doms):
         row = all_ref[d * tps]
         for t in range(1, tps):
@@ -354,18 +331,36 @@
     own = mine[:, prior] + mine[:, step_1] - mine[:, step_0]
     twist_ref[...] = jnp.concatenate([mine[:, step_0], mine[:, step_1]], axis=0)
     normal_ref[...] = own - log_total
-
-
-def normalize(shares, doms, tps, per_dev):
+    for named, copy in copies:
+        pl.when(named)(copy.wait)
+
+
+def finish(own_ancestors, gots, held, shares, step_pairs, doms, tps):
+    per_dev = held.shape[0]
+    count = len(gots)
+    smem = pl.BlockSpec(memory_space=pltpu.SMEM)
+    vmem = pl.BlockSpec(memory_space=pltpu.VMEM)
+    hbm = pl.BlockSpec(memory_space=pl.ANY)
     return pl.pallas_call(
-        functools.partial(normalize_kernel, doms, tps, per_dev),
+        functools.partial(finish_kernel, per_dev, doms, tps, step_pairs),
         out_shape=[
+            jax.ShapeDtypeStruct(held.shape, held.dtype),
             jax.ShapeDtypeStruct((2, per_dev), jnp.float32),
             jax.ShapeDtypeStruct((1, per_dev), jnp.float32),
         ],
-        scratch_shapes=[pltpu.VMEM((doms, HEAD_DIM), jnp.float32)],
-        name="normalize",
-    )(shares)
+        in_specs=[smem] + [vmem] * count + [hbm, vmem],
+        out_specs=[hbm, vmem, vmem],
+        input_output_aliases={1 + count: 0},
+        scratch_shapes=[
+            pltpu.VMEM((doms, HEAD_DIM), jnp.float32),
+            pltpu.SemaphoreType.DMA((count, per_dev)),
+        ],
+        compiler_params=pltpu.CompilerParams(vmem_limit_bytes=VMEM_BYTES),
+        cost_estimate=pl.CostEstimate(
+            flops=0, bytes_accessed=held.size, transcendentals=0
+        ),
+        name="finish",
+    )(own_ancestors, *gots, held, shares)
 
 
 def routes(doms, tps, steps):
@@ -395,13 +390,12 @@
     step_pairs = list(zip(*ORDERS))
     everyone = ("dom", "tp")
 
-    *first_sends, new_lengths, own_lengths = pack(
-        lengths, ancestors, new_kv, gen_cache, doms, step_pairs[:1]
-    )
-    *later_sends, _, _ = pack(lengths, ancestors, new_kv, gen_cache, doms, step_pairs[1:])
+    *sends, new_lengths, own_lengths, own_ancestors = pack(
+        lengths, ancestors, new_kv, gen_cache, doms, step_pairs
+    )
     arrivals = [
         lax.ppermute(send, everyone, routes(doms, tps, steps))
-        for send, steps in zip(first_sends + later_sends, step_pairs)
+        for send, steps in zip(sends, step_pairs)
     ]
 
     bias = jnp.take(twist_bias, tokens, axis=0).reshape(-1)
@@ -410,20 +404,19 @@
     extra = jnp.pad(extra, (0, HEAD_DIM - extra.size))[None]
     shares, resampled = attend(
         own_lengths,
-        ancestors,
+        own_ancestors,
         queries,
-        prompt_kv,
-        gen_cache,
+        in_hbm(prompt_kv),
+        in_hbm(gen_cache),
         new_kv,
         twist_vector,
         extra,
         doms * tps,
     )
     shares = lax.all_to_all(shares, everyone, 0, 0, tiled=True)
-    twist, normalized = normalize(shares, doms, tps, per_dev)
-
-    for got, steps in zip(arrivals, step_pairs):
-        resampled = deliver(ancestors, got, resampled, steps, doms)
+    resampled, twist, normalized = finish(
+        own_ancestors, arrivals, resampled, shares, step_pairs, doms, tps
+    )
     return (twist, normalized.reshape(per_dev), resampled, new_lengths)
 
 

time: 59.4 us -> 51.5 us (0.87)
  Pallas kernels: 28.9 us -> 23.1 us
  local copies, waits for them, and re-layouts: 3.23 us -> 0.99 us
    pallas_call x5 -> x1, Pallas kernels: 6.69 us -> 3.07 us  [finish(): pl.pallas_call(functools.partial(finish_kernel, per_dev, doms, tps, step_...]
    pallas_call x2 -> x1, Pallas kernels: 7.09 us -> 3.77 us  [pack(): pl.pallas_call(functools.partial(pack_kernel, per_dev, doms, step_pairs),...]
    unnamed x20 -> x12, local copies, waits for them, and re-layouts: 2.28 us -> 0.03 us
    pallas_call x1, Pallas kernels: 15.1 us -> 16.3 us  [attend(): pl.pallas_call(functools.partial(attend_kernel, per_dev, group), grid=(kv...]
  transfers between devices with their start and end apart: 4 -> 4, of which waited for: 0 -> 0; matrix products, arithmetic and copies ran while one was open for 2% -> 2% of each run, Pallas kernels for 41% -> 32%
where the time goes in v1:
time: 51.5 us; the launch traced here: 51.2 us
  Pallas kernels  23.1 us (45%)
  blocking collectives  14 us (27%)
  starting transfers between devices  12.3 us (24%)
  local copies, waits for them, and re-layouts  0.99 us (2%)
  between operations  0.76 us (1%)
    pallas_call x1, Pallas kernels, attend(): pl.pallas_call(functools.partial(attend_kernel, per_dev, group), grid=(kv...  16.3 us
    all_to_all x1, blocking collectives, local(): shares = lax.all_to_all(shares, everyone, 0, 0, tiled=True)  14 us
    ppermute x4, starting transfers between devices, local(): lax.ppermute(send, everyone, routes(doms, tps, steps))  12.3 us
    pallas_call x1, Pallas kernels, pack(): pl.pallas_call(functools.partial(pack_kernel, per_dev, doms, step_pairs),...  3.77 us
    pallas_call x1, Pallas kernels, finish(): pl.pallas_call(functools.partial(finish_kernel, per_dev, doms, tps, step_...  3.07 us
  transfers between devices with their start and end apart: 4, of which 0 were waited for; matrix products, arithmetic and copies ran while one was open for 2% of the time, Pallas kernels for 32%

profile of v1, /device:TPU:0, one launch (start us, length us, event | category | flops | bytes accessed | tf_op | source)
XLA Modules:
  0.0 51.2 jit_solution(10600374933011132824)
XLA Ops:
  0.6 0.0 copy-start
  0.6 0.0 copy-start.1
  0.7 0.0 copy-start.4
  0.7 0.0 copy-start.5
  0.7 0.0 copy-start.3
  0.7 0.0 copy-start.2
  0.7 3.8 %pack_sends.1 = (bf16[2,128,1024]{2,1,0:T(8,128)(2,1)}, bf16[2,128,1024]{2,1,0:T(8,128)(2,1)}, bf16[2,128,1024]{2,1,0:T(8,128)(2,1)}, bf16[2,128,1024]{2,1,0:T(8...) custom-call(s32[256]{0:T(256)} %len_hbm.1, s32[256]{0:T(256)} %anc_hbm.1, bf16[2,16,1024]{2,1,0:T(8,128)(2,1)} %new_ref.1, ...), custom_call_target="tpu_custom_call" | custom-call | bytes 4194304 | tf_op jit(solution)/shard_map/pack_sends/pallas_call | solution.py:101
  4.5 1.3 %collective-permute-start = (bf16[2,128,1024]{2,1,0:T(8,128)(2,1)}, bf16[2,128,1024]{2,1,0:T(8,128)(2,1)S(1)}, u32[]{:S(2)}, u32[]{:S(2)}) collective-permute-start(bf16[2,128,1024]{2,1,0:T(8,128)(2,1)} %get-tuple-element.17), channel_id=1, source_target_pairs={{1,3},{3,5},{4,0},{5,7},{6,2},{7,9},{8,4},{9,11},{10,6},{11,13},{1... | collective-permute-start | bytes 1572872 | tf_op jit(solution)/shard_map/ppermute | solution.py:397
  5.8 5.8 %collective-permute-start.1 = (bf16[2,128,1024]{2,1,0:T(8,128)(2,1)}, bf16[2,128,1024]{2,1,0:T(8,128)(2,1)S(1)}, u32[]{:S(2)}, u32[]{:S(2)}) collective-permute-start(bf16[2,128,1024]{2,1,0:T(8,128)(2,1)} %get-tuple-element.18), channel_id=1, source_target_pairs={{0,4},{2,6},{3,1},{4,8},{5,3},{6,10},{7,5},{8,12},{9,7},{10,14},{1... | collective-permute-start | bytes 1572872 | tf_op jit(solution)/shard_map/ppermute | solution.py:397
  11.6 3.9 %collective-permute-start.2 = (bf16[2,128,1024]{2,1,0:T(8,128)(2,1)}, bf16[2,128,1024]{2,1,0:T(8,128)(2,1)S(1)}, u32[]{:S(2)}, u32[]{:S(2)}) collective-permute-start(bf16[2,128,1024]{2,1,0:T(8,128)(2,1)} %get-tuple-element.19), channel_id=1, source_target_pairs={{0,2},{2,4},{4,6},{5,1},{6,8},{7,3},{8,10},{9,5},{10,12},{11,7},{1... | collective-permute-start | bytes 1572872 | tf_op jit(solution)/shard_map/ppermute | solution.py:397
  15.5 1.3 %collective-permute-start.3 = (bf16[2,128,1024]{2,1,0:T(8,128)(2,1)S(1)}, bf16[2,128,1024]{2,1,0:T(8,128)(2,1)S(1)}, u32[]{:S(2)}, u32[]{:S(2)}) collective-permute-start(bf16[2,128,1024]{2,1,0:T(8,128)(2,1)S(1)} %get-tuple-element.20), channel_id=1, source_target_pairs={{1,5},{2,0},{3,7},{4,2},{5,9},{6,4},{7,11},{8,6},{9,13},{10,8},{11... | collective-permute-start | bytes 1572872 | tf_op jit(solution)/shard_map/ppermute | solution.py:397
  16.8 0.0 copy-done.4
  16.8 0.1 reshape.28
  16.9 0.0 copy-done
  16.9 0.7 %gather_fusion = f32[32]{0:T(128)S(1)} fusion(f32[128256]{0:T(1024)S(1)} %copy-done, s32[1024]{0:T(1024)S(1)} %pad_clamp_fusion), kind=kCustom, calls=%fused_computation | custom fusion | bytes 384 | tf_op jit(solution)/shard_map/jit(_take)/gather | solution.py:401
  17.6 0.1 reshape.27
  17.7 0.1 select_n.24
  17.8 0.0 copy-done.5
  17.8 0.1 broadcast_select_fusion
  17.9 0.0 copy-done.1
  17.9 0.0 copy-done.3
  17.9 0.0 copy-done.2
  17.9 16.3 %attend.1 = (f32[32,1,128]{2,1,0:T(1,128)S(1)}, bf16[16,128,1024]{2,1,0:T(8,128)(2,1)}) custom-call(s32[16]{0:T(128)S(1)} %get-tuple-element.21.len_ref, s32[16]{0:T(128)S(1)} %get-tuple-element.16.anc_ref, bf16[2,16,4096]{2,1,0:T(8,128)(2,1)S(1)} %copy-done.2, bf16[4096,1024]{1,0:T(8,128)(2,1)} %prompt_ref.1, bf16[16,128,1024]{2,1,0:T(8,128)(2,1)} %gen_ref.1, ...), custom_call_target="tpu_custom_call" | custom-call | flops 2214592512 | bytes 16777216 | tf_op jit(solution)/shard_map/attend/pallas_call | solution.py:261
  34.2 14.0 %all_to_all.5.refs_5_ = f32[32,1,128]{2,1,0:T(1,128)S(1)} all-to-all(f32[32,1,128]{2,1,0:T(1,128)S(1)} %get-tuple-element.23), channel_id=1, replica_groups=mesh['dom'=16,'tp'=2] {'dom','tp'}, dimensions={0} | all-to-all | bytes 32768 | tf_op jit(solution)/shard_map/all_to_all | solution.py:416
  48.1 0.0 collective-permute-done.refs_0_
  48.1 0.0 collective-permute-done.1.refs_1_
  48.1 0.0 collective-permute-done.2.refs_2_
  48.2 0.0 collective-permute-done.3.refs_3_
  48.2 3.1 %finish.1 = (bf16[16,128,1024]{2,1,0:T(8,128)(2,1)}, f32[2,16]{1,0:T(2,128)}, f32[1,16]{1,0:T(1,128)}) custom-call(s32[16]{0:T(128)S(1)} %get-tuple-element.16.anc_ref, bf16[2,128,1024]{2,1,0:T(8,128)(2,1)S(1)} %collective-permute-done.refs_0_, bf16[2,128,1024]{2,1,0:T(8,128)(2,1)S(1)} %collective-permute-done.1.refs_1_, ...), custom_call_target="tpu_custom_call", output_to_operand_aliasing={{0}: (5, {})} | custom-call | bytes 2097152 | tf_op jit(solution)/shard_map/finish/pallas_call | solution.py:344
  (4 shorter events, 0.0 us)
Async XLA Ops:
  0.6 16.3 %copy-start = (f32[128256]{0:T(1024)S(1)}, f32[128256]{0:T(1024)}, u32[]{:S(2)}) copy-start(f32[128256]{0:T(1024)} %param.18) | copy-start | bytes 1539076
  0.6 17.2 %copy-start.1 = (bf16[2,16,1024]{2,1,0:T(8,128)(2,1)S(1)}, bf16[2,16,1024]{2,1,0:T(8,128)(2,1)}, u32[]{:S(2)}) copy-start(bf16[2,16,1024]{2,1,0:T(8,128)(2,1)} %new_ref.1) | copy-start | bytes 196612
  0.7 16.1 %copy-start.4 = (s32[2,16]{1,0:T(2,128)S(1)}, s32[2,16]{1,0:T(2,128)}, u32[]{:S(2)}) copy-start(s32[2,16]{1,0:T(2,128)} %param.16) | copy-start | bytes 388
  0.7 17.1 %copy-start.5 = (f32[16]{0:T(128)S(1)}, f32[16]{0:T(128)}, u32[]{:S(2)}) copy-start(f32[16]{0:T(128)} %param.19) | copy-start | bytes 196
  0.7 17.2 %copy-start.3 = (f32[4096]{0:T(1024)S(1)}, f32[4096]{0:T(1024)}, u32[]{:S(2)}) copy-start(f32[4096]{0:T(1024)} %param.17) | copy-start | bytes 49156
  0.7 17.2 %copy-start.2 = (bf16[2,16,4096]{2,1,0:T(8,128)(2,1)S(1)}, bf16[2,16,4096]{2,1,0:T(8,128)(2,1)}, u32[]{:S(2)}) copy-start(bf16[2,16,4096]{2,1,0:T(8,128)(2,1)} %q_ref.1) | copy-start | bytes 786436
  4.5 43.7 %collective-permute-start = (bf16[2,128,1024]{2,1,0:T(8,128)(2,1)}, bf16[2,128,1024]{2,1,0:T(8,128)(2,1)S(1)}, u32[]{:S(2)}, u32[]{:S(2)}) collective-permute-start(bf16[2,128,1024]{2,1,0:T(8,128)(2,1)} %get-tuple-element.17), channel_id=1, source_target_pairs={{1,3},{3,5},{4,0},{5,7},{6,2},{7,9},{8,4},{9,11},{10,6},{11,13},{1... | collective-permute-start | bytes 1572872 | tf_op jit(solution)/shard_map/ppermute | solution.py:397
  5.8 42.4 %collective-permute-start.1 = (bf16[2,128,1024]{2,1,0:T(8,128)(2,1)}, bf16[2,128,1024]{2,1,0:T(8,128)(2,1)S(1)}, u32[]{:S(2)}, u32[]{:S(2)}) collective-permute-start(bf16[2,128,1024]{2,1,0:T(8,128)(2,1)} %get-tuple-element.18), channel_id=1, source_target_pairs={{0,4},{2,6},{3,1},{4,8},{5,3},{6,10},{7,5},{8,12},{9,7},{10,14},{1... | collective-permute-start | bytes 1572872 | tf_op jit(solution)/shard_map/ppermute | solution.py:397
  11.6 36.6 %collective-permute-start.2 = (bf16[2,128,1024]{2,1,0:T(8,128)(2,1)}, bf16[2,128,1024]{2,1,0:T(8,128)(2,1)S(1)}, u32[]{:S(2)}, u32[]{:S(2)}) collective-permute-start(bf16[2,128,1024]{2,1,0:T(8,128)(2,1)} %get-tuple-element.19), channel_id=1, source_target_pairs={{0,2},{2,4},{4,6},{5,1},{6,8},{7,3},{8,10},{9,5},{10,12},{11,7},{1... | collective-permute-start | bytes 1572872 | tf_op jit(solution)/shard_map/ppermute | solution.py:397
  15.5 32.7 %collective-permute-start.3 = (bf16[2,128,1024]{2,1,0:T(8,128)(2,1)S(1)}, bf16[2,128,1024]{2,1,0:T(8,128)(2,1)S(1)}, u32[]{:S(2)}, u32[]{:S(2)}) collective-permute-start(bf16[2,128,1024]{2,1,0:T(8,128)(2,1)S(1)} %get-tuple-element.20), channel_id=1, source_target_pairs={{1,5},{2,0},{3,7},{4,2},{5,9},{6,4},{7,11},{8,6},{9,13},{10,8},{11... | collective-permute-start | bytes 1572872 | tf_op jit(solution)/shard_map/ppermute | solution.py:397
